TPU v7x, 32 devices: a whole 2x2x4 slice. The times are simulated.
32 devices in a mesh: tab: 4 (over y, core), row: 8 (over z, x).
Axes of the slice: x: 2, y: 2, z: 4, core: 2. Of those that a mesh axis runs over, the one named last changes fastest.
Arguments:
- ctx_feat: bfloat16 [8, 100, 2048], P('tab', None, 'row'), may hold values from -24 to 24
- qry_feat: bfloat16 [8, 100, 512], P('tab', None, 'row'), may hold values from -24 to 24
- feat_count: int32 [8], P('tab'), may hold values from 3 to 100, as said below
- ctx_count: int32 [8], P('tab'), may hold values from 1024 to 2048, as said below
- qry_count: int32 [8], P('tab'), may hold values from 256 to 512, as said below
- w_emb: bfloat16 [100, 768], replicated, may hold values from -0.625 to 0.625
- ln1_gain: float32 [768], replicated, may hold values from 0.1 to 1.9
- ln1_bias: float32 [768], replicated, may hold values from -3 to 3
- w_qkv: bfloat16 [768, 2304], replicated, may hold values from -0.21875 to 0.21875
- w_out: bfloat16 [768, 768], replicated, may hold values from -6 to 6
- ln2_gain: float32 [768], replicated, may hold values from 0.1 to 1.9
- ln2_bias: float32 [768], replicated, may hold values from -3 to 3
- w_up: bfloat16 [768, 3072], replicated, may hold values from -0.21875 to 0.21875
- b_up: float32 [3072], replicated, may hold values from -3 to 3
- w_down: bfloat16 [3072, 768], replicated, may hold values from -0.109375 to 0.109375
- ctx_cot: bfloat16 [8, 2048, 768], P('tab', 'row'), may hold values from -6 to 6
- qry_cot: bfloat16 [8, 512, 768], P('tab', 'row'), may hold values from -6 to 6
Outputs:
- ctx_out: bfloat16 [8, 2048, 768], P('tab', 'row')
- qry_out: bfloat16 [8, 512, 768], P('tab', 'row')
- ctx_feat_grad: bfloat16 [8, 100, 2048], P('tab', None, 'row')
- qry_feat_grad: bfloat16 [8, 100, 512], P('tab', None, 'row')
- grad_w_emb: float32 [100, 768], replicated
- grad_ln1_gain: float32 [768], P('row')
- grad_ln1_bias: float32 [768], P('row')
- grad_w_qkv: float32 [768, 2304], P('row')
- grad_w_out: float32 [768, 768], P('row')
- grad_ln2_gain: float32 [768], P('row')
- grad_ln2_bias: float32 [768], P('row')
- grad_w_up: float32 [768, 3072], P('row')
- grad_b_up: float32 [3072], P('row')
- grad_w_down: float32 [3072, 768], P('row')
- rms: float32 [4], replicated
Inputs may be any that keep to these rules, and one draw needn't show every extreme that they name: `feat_count`: some table has all 100 slots real. `ctx_count`: among the 2 tables of each index of tab one has all 2048 context rows live. `qry_count`: among the 2 tables of each index of tab one has all 512 query rows live.
All inputs are finite; a program needn't handle non-finite values.
Results may differ from a plain program's by a relative error of at most 0.02.
Values may be sent and summed in bfloat16 or wider, within the bound.
A program may use at most 320 MiB of HBM per device.

v0:
```python
import math

import jax
import jax.numpy as jnp
from jax import lax
from jax.sharding import PartitionSpec as P

HEAD_DIM = 64


EPS = 1e-05
NEGATIVE = -1e30


def standardize(values):
    center = values - jnp.mean(values, axis=-1, keepdims=True)
    inverse = lax.rsqrt(jnp.mean(center * center, axis=-1, keepdims=True) + EPS)
    return (center * inverse, inverse)


def norm_back(grad_out, normed, inverse, gain):
    scaled = grad_out * gain
    inner = (
        scaled
        - jnp.mean(scaled, axis=-1, keepdims=True)
        - normed * jnp.mean(scaled * normed, axis=-1, keepdims=True)
    )
    grad_gain = jnp.sum(grad_out * normed, axis=(0, 1))
    grad_bias = jnp.sum(grad_out, axis=(0, 1))
    return (inverse * inner, grad_gain, grad_bias)


def gelu_exact(values):
    return jax.nn.gelu(values, approximate=False)


def block_scores(query_heads, key_rows, block_index, block_width, key_count, score_scale):
    table_count, local_rows, head_count, head_size = query_heads.shape
    dmodel = head_count * head_size
    block = lax.dynamic_slice_in_dim(key_rows, block_index * block_width, block_width, 1)
    key_block = block[..., :dmodel].reshape(table_count, block_width, head_count, head_size)
    value_block = block[..., dmodel:].reshape(table_count, block_width, head_count, head_size)
    scores = (
        jnp.einsum("trhe,tkhe->thrk", query_heads, key_block, preferred_element_type=jnp.float32)
        * score_scale
    )
    position = block_index * block_width + jnp.arange(block_width)
    live_keys = position[None, :] < key_count[:, None]
    scores = jnp.where(live_keys[:, None, None, :], scores, NEGATIVE)
    return (scores, key_block, value_block)


def local(
    ctx_feat,
    qry_feat,
    feat_count,
    ctx_count,
    qry_count,
    w_emb,
    ln1_gain,
    ln1_bias,
    w_qkv,
    w_out,
    ln2_gain,
    ln2_bias,
    w_up,
    b_up,
    w_down,
    ctx_cot,
    qry_cot,
):
    table_count, slot_count, ctx_rows = ctx_feat.shape
    qry_rows = qry_feat.shape[2]
    local_rows = ctx_rows + qry_rows
    dmodel = w_out.shape[0]
    head_count = dmodel // HEAD_DIM
    score_scale = HEAD_DIM ** (-0.5)
    total_ctx = ctx_rows * lax.axis_size("row")
    row_index = lax.axis_index("row")
    slot_live = (jnp.arange(slot_count)[None, :] < feat_count[:, None]).astype(jnp.bfloat16)
    features = jnp.concatenate([ctx_feat, qry_feat], axis=2) * slot_live[:, :, None]
    ctx_live = (row_index * ctx_rows + jnp.arange(ctx_rows))[None, :] < ctx_count[:, None]
    qry_live = (row_index * qry_rows + jnp.arange(qry_rows))[None, :] < qry_count[:, None]
    valid = jnp.concatenate([ctx_live, qry_live], axis=1).astype(jnp.float32)[..., None]
    embed = jnp.einsum("tfr,fd->trd", features, w_emb, preferred_element_type=jnp.float32)
    normed1, inverse1 = standardize(embed)
    attn_in = (normed1 * ln1_gain + ln1_bias).astype(jnp.bfloat16)
    w_query = w_qkv[:, :dmodel]
    w_pair = w_qkv[:, dmodel:]
    query = jnp.einsum("trd,de->tre", attn_in, w_query, preferred_element_type=jnp.float32).astype(
        jnp.bfloat16
    )
    pairs = jnp.einsum(
        "trd,de->tre", attn_in[:, :ctx_rows], w_pair, preferred_element_type=jnp.float32
    ).astype(jnp.bfloat16)
    gathered = lax.all_gather(pairs, "row", axis=1, tiled=True)
    block_width = math.gcd(total_ctx, 512)
    block_total = total_ctx // block_width
    query_heads = query.reshape(table_count, local_rows, head_count, HEAD_DIM)

    def attend_step(carried, block_index):
        running_max, running_sum, summed = carried
        scores, _, value_block = block_scores(
            query_heads, gathered, block_index, block_width, ctx_count, score_scale
        )
        new_max = jnp.maximum(running_max, jnp.max(scores, axis=-1))
        factor = jnp.exp(running_max - new_max)
        weights = jnp.exp(scores - new_max[..., None])
        running_sum = running_sum * factor + jnp.sum(weights, axis=-1)
        summed = summed * jnp.transpose(factor, (0, 2, 1))[..., None] + jnp.einsum(
            "thrk,tkhe->trhe",
            weights.astype(jnp.bfloat16),
            value_block,
            preferred_element_type=jnp.float32,
        )
        return ((new_max, running_sum, summed), None)

    initial = jnp.full((table_count, head_count, local_rows), NEGATIVE, jnp.float32)
    start_sum = jnp.zeros((table_count, local_rows, head_count, HEAD_DIM), jnp.float32)
    (running_max, running_sum, summed), _ = lax.scan(
        attend_step, (initial, jnp.zeros_like(initial), start_sum), jnp.arange(block_total)
    )
    log_total = running_max + jnp.log(running_sum)
    attended = summed / jnp.transpose(running_sum, (0, 2, 1))[..., None]
    attn_low = attended.reshape(table_count, local_rows, dmodel).astype(jnp.bfloat16)
    branch = jnp.einsum("trd,de->tre", attn_low, w_out, preferred_element_type=jnp.float32)
    mixed = embed + branch
    normed2, inverse2 = standardize(mixed)
    mlp_in = (normed2 * ln2_gain + ln2_bias).astype(jnp.bfloat16)
    hidden = jnp.einsum("trd,de->tre", mlp_in, w_up, preferred_element_type=jnp.float32) + b_up
    activation, gelu_back = jax.vjp(gelu_exact, hidden)
    act_low = activation.astype(jnp.bfloat16)
    mlp = jnp.einsum("tre,ed->trd", act_low, w_down, preferred_element_type=jnp.float32)
    output = (mixed + mlp) * valid
    ctx_out = output[:, :ctx_rows].astype(jnp.bfloat16)
    qry_out = output[:, ctx_rows:].astype(jnp.bfloat16)
    squares = jnp.stack(
        [
            jnp.sum(valid * embed * embed),
            jnp.sum(valid * branch * branch),
            jnp.sum(valid * mlp * mlp),
            jnp.sum(valid * output * output),
        ]
    )
    live_rows = jnp.sum(valid)
    cotangent = jnp.concatenate([ctx_cot, qry_cot], axis=1)
    d_mlp = cotangent * valid.astype(jnp.bfloat16)
    grad_w_down = jnp.einsum("tre,trd->ed", act_low, d_mlp, preferred_element_type=jnp.float32)
    d_act = jnp.einsum("trd,ed->tre", d_mlp, w_down, preferred_element_type=jnp.float32)
    d_hidden = gelu_back(d_act)[0].astype(jnp.bfloat16)
    grad_b_up = jnp.sum(d_hidden.astype(jnp.float32), axis=(0, 1))
    grad_w_up = jnp.einsum("trd,tre->de", mlp_in, d_hidden, preferred_element_type=jnp.float32)
    d_mlp_in = jnp.einsum("tre,de->trd", d_hidden, w_up, preferred_element_type=jnp.float32)
    d_norm2, grad_ln2_gain, grad_ln2_bias = norm_back(d_mlp_in, normed2, inverse2, ln2_gain)
    d_mixed = d_mlp.astype(jnp.float32) + d_norm2
    d_branch = d_mixed.astype(jnp.bfloat16)
    grad_w_out = jnp.einsum("trd,tre->de", attn_low, d_branch, preferred_element_type=jnp.float32)
    d_attn = jnp.einsum("tre,de->trd", d_branch, w_out, preferred_element_type=jnp.float32).astype(
        jnp.bfloat16
    )
    d_attn_heads = d_attn.reshape(table_count, local_rows, head_count, HEAD_DIM)
    dots_rows = jnp.sum(d_attn_heads.astype(jnp.float32) * attended, axis=-1)
    row_dots = jnp.transpose(dots_rows, (0, 2, 1))

    def query_part(block_index):
        scores, key_block, value_block = block_scores(
            query_heads, gathered, block_index, block_width, ctx_count, score_scale
        )
        softened = jnp.exp(scores - log_total[..., None])
        d_soft = jnp.einsum(
            "trhe,tkhe->thrk", d_attn_heads, value_block, preferred_element_type=jnp.float32
        )
        d_scores = (softened * (d_soft - row_dots[..., None])).astype(jnp.bfloat16)
        d_part = (
            jnp.einsum("thrk,tkhe->trhe", d_scores, key_block, preferred_element_type=jnp.float32)
            * score_scale
        )
        return (softened, d_scores, d_part)

    start_query = jnp.zeros((table_count, local_rows, head_count, HEAD_DIM), jnp.float32)

    def grad_step(carried, block_index):
        d_query, d_pairs = carried
        softened, d_scores, d_part = query_part(block_index)
        d_values = jnp.einsum(
            "thrk,trhe->tkhe",
            softened.astype(jnp.bfloat16),
            d_attn_heads,
            preferred_element_type=jnp.float32,
        )
        d_keys = (
            jnp.einsum("thrk,trhe->tkhe", d_scores, query_heads, preferred_element_type=jnp.float32)
            * score_scale
        )
        grad_block = jnp.concatenate(
            [
                d_keys.reshape(table_count, block_width, dmodel),
                d_values.reshape(table_count, block_width, dmodel),
            ],
            axis=-1,
        )
        d_pairs = lax.dynamic_update_slice_in_dim(d_pairs, grad_block, block_index * block_width, 1)
        return ((d_query + d_part, d_pairs), None)

    start_pairs = jnp.zeros((table_count, total_ctx, 2 * dmodel), jnp.float32)
    (d_query, d_pairs), _ = lax.scan(grad_step, (start_query, start_pairs), jnp.arange(block_total))
    own_pairs = lax.psum_scatter(d_pairs, "row", scatter_dimension=1, tiled=True).astype(
        jnp.bfloat16
    )
    d_q = d_query.reshape(table_count, local_rows, dmodel).astype(jnp.bfloat16)
    grad_w_qkv = jnp.concatenate(
        [
            jnp.einsum("trd,tre->de", attn_in, d_q, preferred_element_type=jnp.float32),
            jnp.einsum(
                "trd,tre->de", attn_in[:, :ctx_rows], own_pairs, preferred_element_type=jnp.float32
            ),
        ],
        axis=1,
    )
    d_from_query = jnp.einsum("tre,de->trd", d_q, w_query, preferred_element_type=jnp.float32)
    d_from_pairs = jnp.einsum("tre,de->trd", own_pairs, w_pair, preferred_element_type=jnp.float32)
    d_attn_in = jnp.concatenate(
        [d_from_query[:, :ctx_rows] + d_from_pairs, d_from_query[:, ctx_rows:]], axis=1
    )
    d_norm1, grad_ln1_gain, grad_ln1_bias = norm_back(d_attn_in, normed1, inverse1, ln1_gain)
    d_embed = (d_mixed + d_norm1).astype(jnp.bfloat16)
    grad_w_emb = jnp.einsum("tfr,trd->fd", features, d_embed, preferred_element_type=jnp.float32)
    d_features = jnp.einsum("trd,fd->tfr", d_embed, w_emb, preferred_element_type=jnp.float32)
    d_features = (d_features * slot_live[:, :, None].astype(jnp.float32)).astype(jnp.bfloat16)
    ctx_feat_grad = d_features[:, :, :ctx_rows]
    qry_feat_grad = d_features[:, :, ctx_rows:]
    (
        qkv_part,
        out_part,
        up_part,
        down_part,
        gain1_part,
        bias1_part,
        gain2_part,
        bias2_part,
        upbias_part,
    ) = (
        lax.psum_scatter(grad_w_qkv, "row", scatter_dimension=0, tiled=True),
        lax.psum_scatter(grad_w_out, "row", scatter_dimension=0, tiled=True),
        lax.psum_scatter(grad_w_up, "row", scatter_dimension=0, tiled=True),
        lax.psum_scatter(grad_w_down, "row", scatter_dimension=0, tiled=True),
        lax.psum_scatter(grad_ln1_gain, "row", scatter_dimension=0, tiled=True),
        lax.psum_scatter(grad_ln1_bias, "row", scatter_dimension=0, tiled=True),
        lax.psum_scatter(grad_ln2_gain, "row", scatter_dimension=0, tiled=True),
        lax.psum_scatter(grad_ln2_bias, "row", scatter_dimension=0, tiled=True),
        lax.psum_scatter(grad_b_up, "row", scatter_dimension=0, tiled=True),
    )
    qkv_all, out_all, up_all, down_all, gain1_all, bias1_all, gain2_all, bias2_all, upbias_all = (
        lax.psum(qkv_part.astype(jnp.bfloat16), "tab").astype(jnp.float32),
        lax.psum(out_part.astype(jnp.bfloat16), "tab").astype(jnp.float32),
        lax.psum(up_part.astype(jnp.bfloat16), "tab").astype(jnp.float32),
        lax.psum(down_part.astype(jnp.bfloat16), "tab").astype(jnp.float32),
        lax.psum(gain1_part.astype(jnp.bfloat16), "tab").astype(jnp.float32),
        lax.psum(bias1_part.astype(jnp.bfloat16), "tab").astype(jnp.float32),
        lax.psum(gain2_part.astype(jnp.bfloat16), "tab").astype(jnp.float32),
        lax.psum(bias2_part.astype(jnp.bfloat16), "tab").astype(jnp.float32),
        lax.psum(upbias_part.astype(jnp.bfloat16), "tab").astype(jnp.float32),
    )
    embed_all, squares_all, count_all = lax.psum((grad_w_emb, squares, live_rows), ("tab", "row"))
    rms = jnp.sqrt(squares_all / (count_all * dmodel))
    return (
        ctx_out,
        qry_out,
        ctx_feat_grad,
        qry_feat_grad,
        embed_all,
        gain1_all,
        bias1_all,
        qkv_all,
        out_all,
        gain2_all,
        bias2_all,
        up_all,
        upbias_all,
        down_all,
        rms,
    )


def solution(mesh):
    in_specs = (
        P("tab", None, "row"),
        P("tab", None, "row"),
        P("tab"),
        P("tab"),
        P("tab"),
        P(),
        P(),
        P(),
        P(),
        P(),
        P(),
        P(),
        P(),
        P(),
        P(),
        P("tab", "row", None),
        P("tab", "row", None),
    )
    out_specs = (
        P("tab", "row", None),
        P("tab", "row", None),
        P("tab", None, "row"),
        P("tab", None, "row"),
        P(),
        P("row"),
        P("row"),
        P("row", None),
        P("row", None),
        P("row"),
        P("row"),
        P("row", None),
        P("row"),
        P("row", None),
        P(),
    )
    return jax.shard_map(local, mesh=mesh, in_specs=in_specs, out_specs=out_specs, check_vma=False)
```

profile of v0, /device:TPU:8, one launch (start us, length us, event | category | flops | bytes accessed | tf_op | source)
XLA Modules:
  0.0 1659.3 jit_solution(4493222091648056671)
XLA Ops:
  20.9 172.6 %all-gather.2.cloned.1.call-done = bf16[2,2048,1536]{2,1,0:T(8,128)(2,1)} async-done(((bf16[2,256,1536]{2,1,0:T(8,128)(2,1)}), bf16[2,2048,1536]{2,1,0:T(8,128)(2,1)}) %all-gather.2.cloned.1.call-update) | async-done | bytes 12582928 | tf_op jit(solution)/shard_map/all_gather | solution.py:96
  193.5 15.8 copy.74
  209.2 65.3 %while.28 = (s32[]{:T(128)}, f32[2,12,320]{2,1,0:T(8,128)S(1)}, f32[2,12,320]{2,1,0:T(8,128)S(1)}, f32[2,320,12,64]{1,3,2,0:T(8,128)}, s32[4]{0:T(128)S(1)}, /*i...) while((s32[]{:T(128)}, f32[2,12,320]{2,1,0:T(8,128)S(1)}, ...), condition=%wide.region_5.6_spmd.clone, body=%wide.region_2.5_spmd.clone.sunk | while | flops 1051408896 | bytes 77766936 | solution.py:120
  278.4 8.3 fusion.44
  286.8 19.3 %multiply_convert_fusion.1 = (bf16[2,320,3072]{2,1,0:T(8,128)(2,1)}, f32[2,320,3072]{2,1,0:T(8,128)}) fusion(f32[2,320,3072]{2,1,0:T(8,128)S(1)} %get-tuple-element.366, f32[3072]{0:T(1024)S(1)} %copy-done.43, u8[320,3072]{1,0:T(8,128)(4,1)S(1)} %get-tuple-element.277, u8[320,3072]{1,0:T(8,128)(4,1)S(1)} %get-tuple-element.276), kind=kLoop, calls=%fused_computation.44 | loop fusion | flops 139591680 | bytes 21639168 | tf_op jit(solution)/shard_map/convert_element_type | solution.py:132
  306.1 11.4 convert_reduce_fusion
  317.5 6.9 fusion.28
  324.5 8.1 fusion.41
  338.5 11.5 broadcast_in_dim.33
  350.0 139.9 %while.29 = (s32[]{:T(128)}, f32[2,320,12,64]{1,3,2,0:T(8,128)}, f32[2,2048,1536]{1,2,0:T(8,128)}, s32[4]{0:T(128)S(1)}, bf16[2,2048,1536]{1,2,0:T(8,128)(2,1)},...) while((s32[]{:T(128)}, f32[2,320,12,64]{1,3,2,0:T(8,128)}, ...), condition=%wide.region_12.13_spmd.clone, body=%wide.region_11.12_spmd.clone.sunk | while | flops 2559739392 | bytes 184124720 | solution.py:206
  356.1 5.4 copy-done.2
  366.4 8.5 multiply_convert_fusion.3
  389.7 5.4 copy-done.2
  400.1 8.5 multiply_convert_fusion.3
  408.6 5.5 bitcast_add_fusion.5
  425.1 5.4 copy-done.2
  435.5 8.5 multiply_convert_fusion.3
  444.0 5.4 bitcast_add_fusion.5
  460.4 5.4 copy-done.2
  470.8 8.5 multiply_convert_fusion.3
  479.3 5.4 bitcast_add_fusion.5
  495.5 8.6 convolution_bitcast_fusion.1
  505.2 9.0 convolution_bitcast_fusion
  517.5 375.2 %reduce-scatter.6.cloned.1.call-done = f32[2,256,1536]{1,2,0:T(8,128)} async-done(((f32[2,2048,1536]{1,2,0:T(8,128)}), f32[2,256,1536]{1,2,0:T(8,128)}) %reduce-scatter.6.cloned.1.call-update) | async-done | bytes 3145744 | tf_op jit(solution)/shard_map/reduce_scatter | solution.py:207
  908.5 57.2 %reduce-scatter.10.cloned.1.call-done = f32[96,768]{1,0:T(8,128)} async-done(((f32[768,768]{1,0:T(8,128)}), f32[96,768]{1,0:T(8,128)}) %reduce-scatter.10.cloned.1.call-update) | async-done | bytes 294928 | tf_op jit(solution)/shard_map/reduce_scatter | solution.py:244
  967.3 163.7 %reduce-scatter.12.cloned.1.call-done = f32[96,3072]{1,0:T(8,128)} async-done(((f32[768,3072]{1,0:T(8,128)}), f32[96,3072]{1,0:T(8,128)}) %reduce-scatter.12.cloned.1.call-update) | async-done | bytes 1179664 | tf_op jit(solution)/shard_map/reduce_scatter | solution.py:245
  1133.1 163.9 %reduce-scatter.14.cloned.1.call-done = f32[384,768]{1,0:T(8,128)} async-done(((f32[3072,768]{1,0:T(8,128)}), f32[384,768]{1,0:T(8,128)}) %reduce-scatter.14.cloned.1.call-update) | async-done | bytes 1179664 | tf_op jit(solution)/shard_map/reduce_scatter | solution.py:246
  1309.7 119.3 %reduce-scatter.8.cloned.1.call-done = f32[96,2304]{1,0:T(8,128)} async-done(((f32[768,2304]{1,0:T(8,128)}), f32[96,2304]{1,0:T(8,128)}) %reduce-scatter.8.cloned.1.call-update) | async-done | bytes 884752 | tf_op jit(solution)/shard_map/reduce_scatter | solution.py:243
  1431.1 40.9 %all-reduce.5 = (f32[4]{0:T(128)}, f32[]{:T(128)}) all-reduce(f32[4]{0:T(128)S(1)} %pad_maximum_fusion.2, f32[]{:T(128)} %fusion.70), channel_id=1, replica_groups=mesh['tab'=4,'row'=8] {'tab','row'}, use_global_device_ids=true, to_apply=%region_45.46 | all-reduce | flops 5 | bytes 40 | tf_op jit(solution)/shard_map/psum | solution.py:264
  1475.9 34.3 %all-reduce.6 = (bf16[768]{0:T(1024)(128)(2,1)S(1)}, bf16[768]{0:T(1024)(128)(2,1)S(1)}, bf16[768]{0:T(1024)(128)(2,1)S(1)}, bf16[768]{0:T(1024)(128)(2,1)S(1)}, bf16[3072]{0:T(1024)(128)(2,1)S(1)}) all-reduce(f32[768]{0:T(1024)S(1)} %get-tuple-element.280, ...), channel_id=3, replica_groups=mesh['tab'=4,'row'=8] {'row'}, use_global_device_ids=true, to_apply=%region_18.19.clone | all-reduce | flops 6144 | bytes 36864
  1510.6 5.6 all-reduce.7
  1530.9 119.4 %all-reduce.12.cloned.1.call-done = f32[100,768]{1,0:T(8,128)} async-done(((f32[100,768]{1,0:T(8,128)}), f32[100,768]{1,0:T(8,128)}) %all-reduce.12.cloned.1.call-update) | async-done | bytes 307216 | tf_op jit(solution)/shard_map/psum | solution.py:264
  (314 shorter events, 212.6 us)
Async XLA Ops:
  7.2 269.5 %copy-start = (bf16[768,768]{1,0:T(8,128)(2,1)S(1)}, bf16[768,768]{1,0:T(8,128)(2,1)}, u32[]{:S(2)}) copy-start(bf16[768,768]{1,0:T(8,128)(2,1)} %param.30) | copy-start | bytes 3538948
  7.2 7.2 copy-start.41
  7.2 7.2 copy-start.49
  7.2 186.2 %all-gather.2.cloned.1.call-start = ((), (), s32[]{:S(2)}) async-start(), calls=%async_computation.5 | async-start | bytes 14155776 | tf_op jit(solution)/shard_map/all_gather | solution.py:96
  17.6 875.1 %reduce-scatter.6.cloned.1.call-start = ((), (), s32[]{:S(2)}) async-start(), calls=%async_computation.6 | async-start | bytes 28311552 | tf_op jit(solution)/shard_map/reduce_scatter | solution.py:207
  20.7 188.6 %copy-start.59 = (s32[64]{0:T(128)}, s32[64]{0:T(128)S(1)}, u32[]{:S(2)}) copy-start(s32[64]{0:T(128)S(1)} %iota_add_fusion.3) | copy-start | bytes 772
  20.7 188.6 %copy-start.52 = (s32[256]{0:T(256)}, s32[256]{0:T(256)S(1)}, u32[]{:S(2)}) copy-start(s32[256]{0:T(256)S(1)} %iota_add_fusion.2) | copy-start | bytes 3076
  20.9 303.6 %copy-start.44 = (f32[2,320]{1,0:T(2,128)}, f32[2,320]{1,0:T(2,128)S(1)}, u32[]{:S(2)}) copy-start(f32[2,320]{1,0:T(2,128)S(1)} %get-tuple-element.360) | copy-start | bytes 7684
  20.9 311.6 %copy-start.47 = (bf16[2,320]{1,0:T(2,128)(2,1)}, bf16[2,320]{1,0:T(2,128)(2,1)S(1)}, u32[]{:S(2)}) copy-start(bf16[2,320]{1,0:T(2,128)(2,1)S(1)} %get-tuple-element.359) | copy-start | bytes 3844
  278.0 54.5 %copy-start.7 = (f32[2,320,768]{2,1,0:T(8,128)}, f32[2,320,768]{2,1,0:T(8,128)S(1)}, u32[]{:S(2)}) copy-start(f32[2,320,768]{2,1,0:T(8,128)S(1)} %get-tuple-element.349) | copy-start | bytes 5898244
  278.0 54.5 %copy-start.25 = (f32[2,320]{1,0:T(2,128)}, f32[2,320]{1,0:T(2,128)S(1)}, u32[]{:S(2)}) copy-start(f32[2,320]{1,0:T(2,128)S(1)} %broadcast_multiply_fusion.4) | copy-start | bytes 7684
  278.4 54.1 %copy-start.29 = (f32[2,320]{1,0:T(2,128)}, f32[2,320]{1,0:T(2,128)S(1)}, u32[]{:S(2)}) copy-start(f32[2,320]{1,0:T(2,128)S(1)} %add_rsqrt_fusion) | copy-start | bytes 7684
  286.8 19.4 %copy-start.21 = (bf16[2,256,768]{2,1,0:T(8,128)(2,1)S(1)}, bf16[2,256,768]{2,1,0:T(8,128)(2,1)}, u32[]{:S(2)}) copy-start(bf16[2,256,768]{2,1,0:T(8,128)(2,1)} %param.36) | copy-start | bytes 2359300
  286.8 19.4 %copy-start.31 = (bf16[2,64,768]{2,1,0:T(8,128)(2,1)S(1)}, bf16[2,64,768]{2,1,0:T(8,128)(2,1)}, u32[]{:S(2)}) copy-start(bf16[2,64,768]{2,1,0:T(8,128)(2,1)} %param.37) | copy-start | bytes 589828
  317.5 6.9 copy-start.16
  490.0 5.4 copy-start.8
  490.0 5.4 copy-start.26
  490.0 5.4 copy-start.28
  490.0 475.6 %reduce-scatter.10.cloned.1.call-start = ((), (), s32[]{:S(2)}) async-start(), calls=%async_computation.9 | async-start | bytes 2654208 | tf_op jit(solution)/shard_map/reduce_scatter | solution.py:244
  495.4 635.6 %reduce-scatter.12.cloned.1.call-start = ((), (), s32[]{:S(2)}) async-start(), calls=%async_computation.10 | async-start | bytes 10616832 | tf_op jit(solution)/shard_map/reduce_scatter | solution.py:245
  504.1 792.9 %reduce-scatter.14.cloned.1.call-start = ((), (), s32[]{:S(2)}) async-start(), calls=%async_computation.11 | async-start | bytes 10616832 | tf_op jit(solution)/shard_map/reduce_scatter | solution.py:246
  514.3 914.8 %reduce-scatter.8.cloned.1.call-start = ((), (), s32[]{:S(2)}) async-start(), calls=%async_computation.8 | async-start | bytes 7962624 | tf_op jit(solution)/shard_map/reduce_scatter | solution.py:243
  899.7 624.2 %all-reduce.14.cloned.1.call-start = ((), (), s32[]{:S(2)}) async-start(), calls=%async_computation.12 | async-start | bytes 3538944 | tf_op jit(solution)/shard_map/psum | solution.py:254
  1299.2 5.9 copy-start.6
  1299.2 5.9 copy-start.37
  1299.2 5.9 copy-start.40
  1299.2 5.9 copy-start.42
  1299.2 5.9 copy-start.45
  1431.0 219.3 %all-reduce.12.cloned.1.call-start = ((), (), s32[]{:S(2)}) async-start(), calls=%async_computation.7 | async-start | bytes 638976 | tf_op jit(solution)/shard_map/psum | solution.py:264
  1474.5 48.9 %copy-start.61 = (f32[4]{0:T(128)S(1)}, f32[4]{0:T(128)}, u32[]{:S(2)}) copy-start(f32[4]{0:T(128)} %get-tuple-element.328) | copy-start | bytes 52
  1520.9 131.1 %copy-start.1 = (bf16[768,768]{1,0:T(8,128)(2,1)S(1)}, bf16[768,768]{1,0:T(8,128)(2,1)}, u32[]{:S(2)}) copy-start(bf16[768,768]{1,0:T(8,128)(2,1)} %param.30) | copy-start | bytes 3538948
  1523.9 5.9 copy-start.24
  (50 other events, 130.1 us)
Sparse Core Ops, SparseCore 0:
  17.7 175.7 all-gather.1
  490.1 402.5 reduce-scatter.5
  896.2 69.4 reduce-scatter.9
  969.1 161.8 reduce-scatter.11
  1134.4 162.5 reduce-scatter.13
  1300.5 128.4 reduce-scatter.7
  1433.0 47.5 all-reduce.13
  1523.5 126.7 all-reduce.11
where the time goes:
time: 1670 us; the launch traced here: 1660 us
  waiting for transfers between devices  1170 us (70%)
  matrix products  197 us (12%)
  local copies, waits for them, and re-layouts  94.9 us (6%)
  other arithmetic  90.7 us (5%)
  blocking collectives  80.8 us (5%)
  between operations  17.3 us (1%)
    reduce_scatter x1, waiting for transfers between devices, local(): lax.psum_scatter(d_pairs, 'row', scatter_dimension=1, tiled=True)  375 us
    all_gather x1, waiting for transfers between devices, local(): gathered = lax.all_gather(pairs, 'row', axis=1, tiled=True)  173 us
    reduce_scatter x1, waiting for transfers between devices, local(): lax.psum_scatter(grad_w_down, 'row', scatter_dimension=0, tiled=True)  164 us
    reduce_scatter x1, waiting for transfers between devices, local(): lax.psum_scatter(grad_w_up, 'row', scatter_dimension=0, tiled=True)  164 us
    psum x1, waiting for transfers between devices, local(): lax.psum((grad_w_emb, squares, live_rows), ('tab', 'row'))  119 us
    reduce_scatter x1, waiting for transfers between devices, local(): lax.psum_scatter(grad_w_qkv, 'row', scatter_dimension=0, tiled=True)  119 us
    reduce_scatter x1, waiting for transfers between devices, local(): lax.psum_scatter(grad_w_out, 'row', scatter_dimension=0, tiled=True)  57.2 us
    psum x1, blocking collectives, local(): lax.psum((grad_w_emb, squares, live_rows), ('tab', 'row'))  40.9 us
  transfers between devices with their start and end apart: 8, of which 7 were waited for; matrix products, arithmetic and copies ran while one was open for 4% of the time, Pallas kernels for 0%

commit v1 on v0

--- a/solution.py
+++ b/solution.py
@@ -1,8 +1,11 @@
+import functools
 import math
 
 import jax
 import jax.numpy as jnp
 from jax import lax
+from jax.experimental import pallas as pl
+from jax.experimental.pallas import tpu as pltpu
 from jax.sharding import PartitionSpec as P
 
 HEAD_DIM = 64
@@ -50,7 +53,7 @@
     return (scores, key_block, value_block)
 
 
-def local(
+def local_by_rows(
     ctx_feat,
     qry_feat,
     feat_count,
@@ -282,6 +285,383 @@
     )
 
 
+MESH = pl.DeviceIdType.MESH
+LANES = 128
+NT = (((1,), (1,)), ((), ()))
+
+
+def swap_rows(values, pick, collective_id):
+    row_size = lax.axis_size("row")
+    block = values.shape[1:]
+
+    def kernel(src, dst, own_sem, send_sem, recv_sem):
+        tab, row = lax.axis_index("tab"), lax.axis_index("row")
+        barrier = pltpu.get_barrier_semaphore()
+        peers = [(tab, lax.rem(row + k, row_size)) for k in range(1, row_size)]
+        for peer in peers:
+            pl.semaphore_signal(barrier, inc=1, device_id=peer, device_id_type=MESH)
+        pl.semaphore_wait(barrier, row_size - 1)
+        copies = []
+        for k, peer in enumerate(peers):
+            copy = pltpu.make_async_remote_copy(
+                src_ref=src.at[pick(peer[1])],
+                dst_ref=dst.at[row],
+                send_sem=send_sem.at[k],
+                recv_sem=recv_sem.at[k],
+                device_id=peer,
+                device_id_type=MESH,
+            )
+            copy.start()
+            copies.append(copy)
+        own = pltpu.make_async_copy(src.at[pick(row)], dst.at[row], own_sem)
+        own.start()
+        own.wait()
+        for copy in copies:
+            copy.wait()
+
+    return pl.pallas_call(
+        kernel,
+        out_shape=jax.ShapeDtypeStruct((row_size,) + block, values.dtype),
+        in_specs=[pl.BlockSpec(memory_space=pl.ANY)],
+        out_specs=pl.BlockSpec(memory_space=pl.ANY),
+        scratch_shapes=[
+            pltpu.SemaphoreType.DMA,
+            pltpu.SemaphoreType.DMA((row_size - 1,)),
+            pltpu.SemaphoreType.DMA((row_size - 1,)),
+        ],
+        compiler_params=pltpu.CompilerParams(collective_id=collective_id, has_side_effects=True),
+        name="swap_rows",
+    )(values)
+
+
+def pack_heads(values):
+    rows, width = values.shape[-2:]
+    whole = width // LANES
+    parts = [values[..., i * LANES : (i + 1) * LANES] for i in range(whole)]
+    if width % LANES:
+        last = values[..., whole * LANES :]
+        parts.append(jnp.concatenate([last[..., : rows // 2, :], last[..., rows // 2 :, :]], axis=-1))
+    return jnp.concatenate(parts, axis=-2)
+
+
+def unpack_heads(packed, rows, width):
+    whole = width // LANES
+    parts = [packed[..., i * rows : (i + 1) * rows, :] for i in range(whole)]
+    if width % LANES:
+        last = packed[..., whole * rows :, :]
+        parts.append(jnp.concatenate([last[..., :HEAD_DIM], last[..., HEAD_DIM:]], axis=-2))
+    return jnp.concatenate(parts, axis=-1)
+
+
+def lane_of(shape):
+    return lax.broadcasted_iota(jnp.int32, shape, len(shape) - 1)
+
+
+def split_three(values):
+    high = values.astype(jnp.bfloat16)
+    rest = values - high.astype(jnp.float32)
+    mid = rest.astype(jnp.bfloat16)
+    tail = (rest - mid.astype(jnp.float32)).astype(jnp.bfloat16)
+    return (high, mid, tail)
+
+
+def set_lanes(values, first, columns):
+    lane = lane_of(values.shape)
+    values = values.astype(jnp.float32)
+    for i, column in enumerate(columns):
+        values = jnp.where(lane == first + i, column.astype(jnp.float32), values)
+    return values.astype(jnp.bfloat16)
+
+
+def attend_kernel(q_ref, k_ref, v_ref, out_ref, back_ref):
+    scores = lax.dot_general(q_ref[0], k_ref[0], NT, preferred_element_type=jnp.float32)
+    top = jnp.max(scores, axis=-1, keepdims=True)
+    weights = jnp.exp(scores - top).astype(jnp.bfloat16)
+    summed = jnp.dot(weights, v_ref[0], preferred_element_type=jnp.float32)
+    total = summed[:, HEAD_DIM : HEAD_DIM + 1]
+    out_ref[0] = (summed / total).astype(jnp.bfloat16)
+    log_total = top + jnp.log(total)
+    back_ref[0] = set_lanes(q_ref[0], HEAD_DIM + 1, split_three(-log_total))
+
+
+def attend(queries, keys, values, block):
+    heads, rows, _ = queries.shape
+    total = keys.shape[1]
+    by_query = pl.BlockSpec((1, block, LANES), lambda h, i: (h, i, 0))
+    by_key = pl.BlockSpec((1, total, LANES), lambda h, i: (h, 0, 0))
+    return pl.pallas_call(
+        attend_kernel,
+        grid=(heads, rows // block),
+        in_specs=[by_query, by_key, by_key],
+        out_specs=[by_query, by_query],
+        out_shape=[jax.ShapeDtypeStruct((heads, rows, LANES), jnp.bfloat16)] * 2,
+        compiler_params=pltpu.CompilerParams(vmem_limit_bytes=48 * 2**20),
+        name="attend",
+    )(queries, keys, values)
+
+
+def attend_back_kernel(chunk, q_ref, k_ref, kt_ref, v_ref, o_ref, g_ref, dq_ref, dk_ref, dv_ref, dk_sum, dv_sum):
+    step = pl.program_id(1)
+
+    @pl.when(step == 0)
+    def _():
+        dk_sum[...] = jnp.zeros_like(dk_sum)
+        dv_sum[...] = jnp.zeros_like(dv_sum)
+
+    query, grad = q_ref[0], g_ref[0]
+    inner = jnp.sum(
+        jnp.where(lane_of(grad.shape) < HEAD_DIM, grad.astype(jnp.float32) * o_ref[0].astype(jnp.float32), 0.0),
+        axis=-1,
+        keepdims=True,
+    )
+    grad = set_lanes(grad, HEAD_DIM, split_three(-inner))
+    total = k_ref.shape[1]
+    d_query = jnp.zeros((HEAD_DIM, query.shape[0]), jnp.float32)
+    for i in range(total // chunk):
+        at = pl.ds(i * chunk, chunk)
+        scores = lax.dot_general(k_ref[0, at], query, NT, preferred_element_type=jnp.float32)
+        probs = jnp.exp(scores)
+        d_probs = lax.dot_general(v_ref[0, at], grad, NT, preferred_element_type=jnp.float32)
+        d_scores = (probs * d_probs).astype(jnp.bfloat16)
+        dv_sum[at] += jnp.dot(probs.astype(jnp.bfloat16), grad, preferred_element_type=jnp.float32)
+        dk_sum[at] += jnp.dot(d_scores, query, preferred_element_type=jnp.float32)
+        d_query += jnp.dot(kt_ref[0, :, at], d_scores, preferred_element_type=jnp.float32)
+    dq_ref[0] = (d_query * HEAD_DIM ** (-0.5)).T.astype(jnp.bfloat16)
+
+    @pl.when(step == pl.num_programs(1) - 1)
+    def _():
+        dk_ref[0] = dk_sum[:, :HEAD_DIM].astype(jnp.bfloat16)
+        dv_ref[0] = dv_sum[:, :HEAD_DIM].astype(jnp.bfloat16)
+
+
+def attend_back(queries, keys, keys_t, values, outs, grads, block, chunk):
+    heads, rows, _ = queries.shape
+    total = keys.shape[1]
+    by_query = pl.BlockSpec((1, block, LANES), lambda h, i: (h, i, 0))
+    by_key = pl.BlockSpec((1, total, LANES), lambda h, i: (h, 0, 0))
+    return pl.pallas_call(
+        functools.partial(attend_back_kernel, chunk),
+        grid=(heads, rows // block),
+        in_specs=[
+            by_query,
+            by_key,
+            pl.BlockSpec((1, HEAD_DIM, total), lambda h, i: (h, 0, 0)),
+            by_key,
+            by_query,
+            by_query,
+        ],
+        out_specs=[
+            pl.BlockSpec((1, block, HEAD_DIM), lambda h, i: (h, i, 0)),
+            pl.BlockSpec((1, total, HEAD_DIM), lambda h, i: (h, 0, 0)),
+            pl.BlockSpec((1, total, HEAD_DIM), lambda h, i: (h, 0, 0)),
+        ],
+        out_shape=[
+            jax.ShapeDtypeStruct((heads, rows, HEAD_DIM), jnp.bfloat16),
+            jax.ShapeDtypeStruct((heads, total, HEAD_DIM), jnp.bfloat16),
+            jax.ShapeDtypeStruct((heads, total, HEAD_DIM), jnp.bfloat16),
+        ],
+        scratch_shapes=[pltpu.VMEM((total, LANES), jnp.float32)] * 2,
+        compiler_params=pltpu.CompilerParams(vmem_limit_bytes=48 * 2**20),
+        name="attend_back",
+    )(queries, keys, keys_t, values, outs, grads)
+
+
+def add_over_tab(part):
+    return lax.psum(part.astype(jnp.bfloat16), "tab").astype(jnp.float32)
+
+
+def scatter_add(grad):
+    part = lax.psum_scatter(grad.astype(jnp.bfloat16), "row", scatter_dimension=0, tiled=True)
+    return add_over_tab(part)
+
+
+def local_by_heads(
+    ctx_feat,
+    qry_feat,
+    feat_count,
+    ctx_count,
+    qry_count,
+    w_emb,
+    ln1_gain,
+    ln1_bias,
+    w_qkv,
+    w_out,
+    ln2_gain,
+    ln2_bias,
+    w_up,
+    b_up,
+    w_down,
+    ctx_cot,
+    qry_cot,
+):
+    table_count, slot_count, ctx_rows = ctx_feat.shape
+    qry_rows = qry_feat.shape[2]
+    local_rows = ctx_rows + qry_rows
+    dmodel = w_out.shape[0]
+    head_count = dmodel // HEAD_DIM
+    score_scale = HEAD_DIM ** (-0.5)
+    row_size = lax.axis_size("row")
+    total_ctx = ctx_rows * row_size
+    all_rows = local_rows * row_size
+    row_index = lax.axis_index("row")
+    groups = row_size // table_count
+    heads = head_count // groups
+    width = heads * HEAD_DIM
+    table, group = row_index // groups, row_index % groups
+
+    slot_live = (jnp.arange(slot_count)[None, :] < feat_count[:, None]).astype(jnp.bfloat16)
+    features = jnp.concatenate([ctx_feat, qry_feat], axis=2) * slot_live[:, :, None]
+    by_row = jnp.pad(jnp.transpose(features, (0, 2, 1)), ((0, 0), (0, 0), (0, LANES - slot_count)))
+    w_emb_pad = jnp.pad(w_emb, ((0, LANES - slot_count), (0, 0)))
+    ctx_live = (row_index * ctx_rows + jnp.arange(ctx_rows))[None, :] < ctx_count[:, None]
+    qry_live = (row_index * qry_rows + jnp.arange(qry_rows))[None, :] < qry_count[:, None]
+    valid = jnp.concatenate([ctx_live, qry_live], axis=1).astype(jnp.float32)[..., None]
+
+    table_feat = swap_rows(by_row, lambda p: p // groups, 0)
+    table_embed = jnp.einsum("prf,fd->prd", table_feat, w_emb_pad, preferred_element_type=jnp.float32)
+    normed1, inverse1 = standardize(table_embed)
+    attn_in = (normed1 * ln1_gain + ln1_bias).astype(jnp.bfloat16)
+    w_three = w_qkv.reshape(dmodel, 3, head_count, HEAD_DIM)
+    w_three = lax.dynamic_slice_in_dim(w_three, group * heads, heads, 2)
+    w_lanes = jnp.pad(w_three, ((0, 0), (0, 0), (0, 0), (0, LANES - HEAD_DIM)))
+    projected = jnp.einsum("prd,dnhe->nhpre", attn_in, w_lanes, preferred_element_type=jnp.float32)
+    lane = jnp.arange(LANES)
+    my_count = lax.dynamic_index_in_dim(ctx_count, table, 0, keepdims=False)
+    live_keys = (jnp.arange(total_ctx) < my_count).reshape(row_size, ctx_rows)
+    bias = jnp.where(live_keys, 0.0, NEGATIVE)[None, :, :, None]
+    queries = jnp.where(lane == HEAD_DIM, 1.0, projected[0] * score_scale).astype(jnp.bfloat16)
+    queries = queries.reshape(heads, all_rows, LANES)
+    keys = jnp.where(lane == HEAD_DIM, bias, projected[1][:, :, :ctx_rows])
+    keys = jnp.where((lane > HEAD_DIM) & (lane < HEAD_DIM + 4), 1.0, keys).astype(jnp.bfloat16)
+    keys = keys.reshape(heads, total_ctx, LANES)
+    values = jnp.where((lane >= HEAD_DIM) & (lane < HEAD_DIM + 3), 1.0, projected[2][:, :, :ctx_rows])
+    values = values.astype(jnp.bfloat16).reshape(heads, total_ctx, LANES)
+    outs, back_queries = attend(queries, keys, values, math.gcd(all_rows, 512))
+
+    def to_rows(by_head):
+        wide = jnp.transpose(by_head[..., :HEAD_DIM], (1, 0, 2)).reshape(row_size, local_rows, width)
+        return swap_rows(pack_heads(wide), lambda p: p, 1)
+
+    packed = to_rows(outs)
+    attn_low = unpack_heads(packed, local_rows, width).reshape(table_count, groups, local_rows, width)
+    attn_low = jnp.transpose(attn_low, (0, 2, 1, 3)).reshape(table_count, local_rows, dmodel)
+
+    embed = jnp.einsum("trf,fd->trd", by_row, w_emb_pad, preferred_element_type=jnp.float32)
+    branch = jnp.einsum("trd,de->tre", attn_low, w_out, preferred_element_type=jnp.float32)
+    mixed = embed + branch
+    normed2, inverse2 = standardize(mixed)
+    mlp_in = (normed2 * ln2_gain + ln2_bias).astype(jnp.bfloat16)
+    hidden = jnp.einsum("trd,de->tre", mlp_in, w_up, preferred_element_type=jnp.float32) + b_up
+    activation, gelu_back = jax.vjp(gelu_exact, hidden)
+    act_low = activation.astype(jnp.bfloat16)
+    mlp = jnp.einsum("tre,ed->trd", act_low, w_down, preferred_element_type=jnp.float32)
+    output = (mixed + mlp) * valid
+    ctx_out = output[:, :ctx_rows].astype(jnp.bfloat16)
+    qry_out = output[:, ctx_rows:].astype(jnp.bfloat16)
+    squares = jnp.stack(
+        [
+            jnp.sum(valid * embed * embed),
+            jnp.sum(valid * branch * branch),
+            jnp.sum(valid * mlp * mlp),
+            jnp.sum(valid * output * output),
+        ]
+    )
+    live_rows = jnp.sum(valid)
+    cotangent = jnp.concatenate([ctx_cot, qry_cot], axis=1)
+    d_mlp = cotangent * valid.astype(jnp.bfloat16)
+    grad_w_down = jnp.einsum("tre,trd->ed", act_low, d_mlp, preferred_element_type=jnp.float32)
+    d_act = jnp.einsum("trd,ed->tre", d_mlp, w_down, preferred_element_type=jnp.float32)
+    d_hidden = gelu_back(d_act)[0].astype(jnp.bfloat16)
+    grad_b_up = jnp.sum(d_hidden.astype(jnp.float32), axis=(0, 1))
+    grad_w_up = jnp.einsum("trd,tre->de", mlp_in, d_hidden, preferred_element_type=jnp.float32)
+    d_mlp_in = jnp.einsum("tre,de->trd", d_hidden, w_up, preferred_element_type=jnp.float32)
+    d_norm2, grad_ln2_gain, grad_ln2_bias = norm_back(d_mlp_in, normed2, inverse2, ln2_gain)
+    d_mixed = d_mlp.astype(jnp.float32) + d_norm2
+    d_branch = d_mixed.astype(jnp.bfloat16)
+    grad_w_out = jnp.einsum("trd,tre->de", attn_low, d_branch, preferred_element_type=jnp.float32)
+    d_attn = jnp.einsum("tre,de->trd", d_branch, w_out, preferred_element_type=jnp.float32).astype(
+        jnp.bfloat16
+    )
+
+    d_attn = jnp.transpose(d_attn.reshape(table_count, local_rows, groups, width), (0, 2, 1, 3))
+    d_attn = d_attn.reshape(row_size, local_rows, width)
+    d_outs = unpack_heads(swap_rows(pack_heads(d_attn), lambda p: p, 2), local_rows, width)
+    d_outs = jnp.transpose(d_outs.reshape(all_rows, heads, HEAD_DIM), (1, 0, 2))
+    d_outs = jnp.pad(d_outs, ((0, 0), (0, 0), (0, LANES - HEAD_DIM)))
+    keys_t = jnp.transpose(keys[..., :HEAD_DIM], (0, 2, 1))
+    d_q, d_k, d_v = attend_back(
+        back_queries, keys, keys_t, values, outs, d_outs, math.gcd(all_rows, 512), math.gcd(total_ctx, 512)
+    )
+    d_q = d_q.reshape(heads, row_size, local_rows, HEAD_DIM)
+    d_k = d_k.reshape(heads, row_size, ctx_rows, HEAD_DIM)
+    d_v = d_v.reshape(heads, row_size, ctx_rows, HEAD_DIM)
+    over_qry = ((0, 0), (0, 0), (0, qry_rows), (0, 0))
+    d_three = jnp.stack([d_q, jnp.pad(d_k, over_qry), jnp.pad(d_v, over_qry)])
+    d_three = jnp.transpose(d_three, (2, 3, 0, 1, 4)).reshape(row_size, local_rows, 3 * width)
+    w_mine = w_three.reshape(dmodel, 3 * width)
+    grad_mine = jnp.einsum("prd,pre->de", attn_in, d_three, preferred_element_type=jnp.float32)
+    d_attn_in = jnp.einsum("pre,de->prd", d_three, w_mine, preferred_element_type=jnp.float32)
+    d_norm1, grad_ln1_gain, grad_ln1_bias = norm_back(d_attn_in, normed1, inverse1, ln1_gain)
+    d_norm1 = d_norm1.astype(jnp.bfloat16)
+    grad_w_emb = jnp.einsum("prf,prd->fd", table_feat, d_norm1, preferred_element_type=jnp.float32)
+    grad_w_emb += jnp.einsum("trf,trd->fd", by_row, d_branch, preferred_element_type=jnp.float32)
+    grad_w_emb = grad_w_emb[:slot_count]
+    feat_terms = jnp.einsum("prd,fd->prf", d_norm1, w_emb_pad, preferred_element_type=jnp.float32)
+    feat_terms = swap_rows(feat_terms.astype(jnp.bfloat16), lambda p: p, 3)
+    feat_terms = feat_terms.reshape(table_count, groups, local_rows, LANES).astype(jnp.float32)
+    own_term = jnp.einsum("trd,fd->trf", d_branch, w_emb_pad, preferred_element_type=jnp.float32)
+    d_features = jnp.transpose(own_term + jnp.sum(feat_terms, axis=1), (0, 2, 1))[:, :slot_count]
+    d_features = (d_features * slot_live[:, :, None].astype(jnp.float32)).astype(jnp.bfloat16)
+    ctx_feat_grad = d_features[:, :, :ctx_rows]
+    qry_feat_grad = d_features[:, :, ctx_rows:]
+
+    shard = dmodel // row_size
+    mine = swap_rows(grad_mine.astype(jnp.bfloat16).reshape(row_size, shard, 3 * width), lambda p: p, 4)
+    mine = jnp.sum(mine.astype(jnp.float32).reshape(table_count, groups, shard, 3, width), axis=0)
+    qkv_all = add_over_tab(jnp.transpose(mine, (1, 2, 0, 3)).reshape(shard, 3 * dmodel))
+    out_all = scatter_add(grad_w_out)
+    up_all = scatter_add(grad_w_up)
+    down_all = scatter_add(grad_w_down)
+    vectors = (grad_ln1_gain, grad_ln1_bias, grad_ln2_gain, grad_ln2_bias, grad_b_up)
+    grad_w_emb, squares, live_rows, vectors = lax.psum(
+        (grad_w_emb, squares, live_rows, vectors), ("tab", "row")
+    )
+    own_parts = [
+        lax.dynamic_slice_in_dim(v, row_index * (v.shape[0] // row_size), v.shape[0] // row_size, 0)
+        for v in vectors
+    ]
+    gain1_all, bias1_all, gain2_all, bias2_all, upbias_all = own_parts
+    rms = jnp.sqrt(squares / (live_rows * dmodel))
+    return (
+        ctx_out,
+        qry_out,
+        ctx_feat_grad,
+        qry_feat_grad,
+        grad_w_emb,
+        gain1_all,
+        bias1_all,
+        qkv_all,
+        out_all,
+        gain2_all,
+        bias2_all,
+        up_all,
+        upbias_all,
+        down_all,
+        rms,
+    )
+
+
+def local(ctx_feat, qry_feat, *rest):
+    table_count, slot_count, ctx_rows = ctx_feat.shape
+    qry_rows = qry_feat.shape[2]
+    head_count = rest[6].shape[0] // HEAD_DIM
+    row_size = lax.axis_size("row")
+    even = row_size % table_count == 0 and head_count % (row_size // table_count) == 0
+    whole = slot_count <= LANES and ctx_rows % LANES == 0 and qry_rows % 32 == 0
+    inner = local_by_heads if even and whole else local_by_rows
+    return inner(ctx_feat, qry_feat, *rest)
+
+
 def solution(mesh):
     in_specs = (
         P("tab", None, "row"),

time: 1670 us -> 705 us (0.42)
  waiting for transfers between devices: 1170 us -> 196 us
  Pallas kernels: 0 us -> 195 us
  matrix products: 197 us -> 102 us
  blocking collectives: 80.8 us -> 42.3 us
  other arithmetic: 90.7 us -> 58.9 us
    reduce_scatter x5 -> x3, waiting for transfers between devices: 879 us -> 106 us  [scatter_add(): lax.psum_scatter(grad.astype(jnp.bfloat16), 'row', scatter_dimension=0, t...]
    pallas_call x0 -> x7, Pallas kernels: none -> 195 us  [the longest x5 110 us: swap_rows(): pl.pallas_call(kernel, out_shape=jax.ShapeDtypeStruct((row_size,) + block...]
    all_gather x1 -> x0, waiting for transfers between devices: 173 us -> none  [local(): gathered = lax.all_gather(pairs, 'row', axis=1, tiled=True)]
    dot_general x46 -> x18, matrix products: 197 us -> 102 us  [the longest x1 19.8 us: local_by_heads(): jnp.einsum('trd,ed->tre', d_mlp, w_down, preferred_element_type=jnp.float32)]
    unnamed x1 -> x0, blocking collectives: 34.3 us -> none
    psum x2, waiting for transfers between devices: 119 us -> 90.2 us  [the longest x1 90.2 us: local_by_heads(): lax.psum((grad_w_emb, squares, live_rows, vectors), ('tab', 'row'))]
    while x36 -> x0, local copies, waits for them, and re-layouts: 27.9 us -> none
    reduce_sum x9 -> x2, other arithmetic: 21.8 us -> 1.83 us  [the longest x1 1.23 us: local_by_heads(): jnp.sum(feat_terms, axis=1)]
  transfers between devices with their start and end apart: 8 -> 5, of which waited for: 7 -> 3; matrix products, arithmetic and copies ran while one was open for 4% -> 15% of each run, Pallas kernels for 0% -> 16%
where the time goes in v1:
time: 705 us; the launch traced here: 694 us
  waiting for transfers between devices  196 us (28%)
  Pallas kernels  195 us (28%)
  matrix products  102 us (14%)
  local copies, waits for them, and re-layouts  82.8 us (12%)
  other arithmetic  58.9 us (8%)
  blocking collectives  42.3 us (6%)
  between operations  15.5 us (2%)
    pallas_call x5, Pallas kernels, swap_rows(): pl.pallas_call(kernel, out_shape=jax.ShapeDtypeStruct((row_size,) + block...  110 us
    reduce_scatter x3, waiting for transfers between devices, scatter_add(): lax.psum_scatter(grad.astype(jnp.bfloat16), 'row', scatter_dimension=0, t...  106 us
    psum x1, waiting for transfers between devices, local_by_heads(): lax.psum((grad_w_emb, squares, live_rows, vectors), ('tab', 'row'))  90.2 us
    pallas_call x1, Pallas kernels, attend_back(): pl.pallas_call(functools.partial(attend_back_kernel, chunk), grid=(heads,...  45.4 us
    psum x1, blocking collectives, local_by_heads(): lax.psum((grad_w_emb, squares, live_rows, vectors), ('tab', 'row'))  42.3 us
    pallas_call x1, Pallas kernels, attend(): pl.pallas_call(attend_kernel, grid=(heads, rows // block), in_specs=[by_q...  39.8 us
    unnamed x142, local copies, waits for them, and re-layouts  30.7 us
    dot_general x1, matrix products, local_by_heads(): jnp.einsum('trd,ed->tre', d_mlp, w_down, preferred_element_type=jnp.float32)  19.8 us
  transfers between devices with their start and end apart: 5, of which 3 were waited for; matrix products, arithmetic and copies ran while one was open for 15% of the time, Pallas kernels for 16%

profile of v1, /device:TPU:8, one launch (start us, length us, event | category | flops | bytes accessed | tf_op | source)
XLA Modules:
  0.0 694.0 jit_solution(11197437073635054280)
XLA Ops:
  7.3 5.9 copy.91
  18.4 18.0 %swap_rows.5 = bf16[8,320,128]{2,1,0:T(8,128)(2,1)} custom-call(bf16[2,320,128]{2,1,0:T(8,128)(2,1)} %pad.23.src), custom_call_target="tpu_custom_call" | custom-call | tf_op jit(solution)/shard_map/swap_rows/pallas_call | solution.py:322
  42.7 6.0 convolution_bitcast_fusion
  48.7 3.4 slice_bitcast_fusion
  56.3 39.8 %attend.1 = (bf16[3,2560,128]{2,1,0:T(8,128)(2,1)S(1)}, bf16[3,2560,128]{2,1,0:T(8,128)(2,1)}) custom-call(bf16[3,2560,128]{2,1,0:T(8,128)(2,1)} %select_convert_fusion.q_ref, bf16[3,2048,128]{2,1,0:T(8,128)(2,1)S(1)} %bitcast.154, bf16[3,2048,128]{2,1,0:T(8,128)(2,1)S(1)} %bitcast.157), custom_call_target="tpu_custom_call" | custom-call | tf_op jit(solution)/shard_map/attend/pallas_call | solution.py:392
  100.0 2.6 copy.95
  102.6 2.8 reshape.302
  114.5 24.6 %swap_rows.6 = bf16[8,480,128]{2,1,0:T(8,128)(2,1)} custom-call(bf16[8,480,128]{2,1,0:T(8,128)(2,1)} %maximum_maximum_fusion.2.src), custom_call_target="tpu_custom_call" | custom-call | tf_op jit(solution)/shard_map/swap_rows/pallas_call | solution.py:322
  142.8 2.5 copy.99
  151.4 8.6 %fusion.27 = (u8[320,3072]{1,0:T(8,128)(4,1)S(1)}, u8[320,3072]{1,0:T(8,128)(4,1)S(1)}, f32[2,320,3072]{2,1,0:T(8,128)S(1)}) fusion(f32[3072]{0:T(1024)S(1)} %copy-done.35, bf16[768,3072]{1,0:T(8,128)(2,1)} %param.29, f32[2,320,768]{2,1,0:T(8,128)} %copy-done.7, f32[768]{0:T(1024)S(1)} %copy-done.57, f32[768]{0:T(1024)S(1)} %copy-done.42, ...), kind=kOutput, calls=%fused_computation.72 | convolution fusion | flops 3047915520 | bytes 16538624 | tf_op jit(solution)/shard_map/trd,de->tre/dot_general | solution.py:554
  160.0 19.2 %multiply_convert_fusion.1 = (bf16[2,320,3072]{2,1,0:T(8,128)(2,1)S(1)}, f32[2,320,3072]{2,1,0:T(8,128)}) fusion(f32[2,320,3072]{2,1,0:T(8,128)S(1)} %get-tuple-element.146, f32[3072]{0:T(1024)S(1)} %copy-done.35, u8[320,3072]{1,0:T(8,128)(4,1)S(1)} %get-tuple-element.88, u8[320,3072]{1,0:T(8,128)(4,1)S(1)} %get-tuple-element.87), kind=kLoop, calls=%fused_computation.17 | loop fusion | flops 139591680 | bytes 21639168 | tf_op jit(solution)/shard_map/convert_element_type | solution.py:556
  179.3 8.3 %fusion.10 = f32[2,320,768]{2,1,0:T(8,128)} fusion(bf16[2,320,3072]{2,1,0:T(8,128)(2,1)S(1)} %get-tuple-element.119, bf16[3072,768]{1,0:T(8,128)(2,1)} %param.31), kind=kOutput, calls=%fused_computation.36 | convolution fusion | flops 3019898880 | bytes 10616832 | tf_op jit(solution)/shard_map/tre,ed->trd/dot_general | solution.py:557
  187.6 19.8 %convert_reduce_fusion = (f32[3072]{0:T(1024)}, bf16[2,320,3072]{2,1,0:T(8,128)(2,1)}) fusion(f32[2,320,3072]{2,1,0:T(8,128)} %get-tuple-element.120, bf16[3072,768]{1,0:T(8,128)(2,1)} %param.31, bf16[2,64,768]{2,1,0:T(8,128)(2,1)S(1)} %copy-done.29, bf16[2,256,768]{2,1,0:T(8,128)(2,1)S(1)} %copy-done.28, bf16[2,320]{1,0:T(2,128)(2,1)S(1)} %get-tuple-element.139, ...), kind=kOutput, calls=%fused_computation.13 | convolution fusion | flops 3056268288 | bytes 25388288 | tf_op jit(solution)/shard_map/trd,ed->tre/dot_general | solution.py:573
  207.5 10.7 %fusion.22 = (f32[]{:T(128)}, f32[]{:T(128)}, f32[768]{0:T(1024)}, f32[768]{0:T(1024)}, f32[2,320]{1,0:T(2,128)S(1)}, /*index=5*/f32[2,320]{1,0:T(2,128)S(1)}, f...) fusion(f32[2,320,768]{2,1,0:T(8,128)} %get-tuple-element.145, ...), kind=kOutput, calls=%fused_computation.59 | convolution fusion | flops 3031692800 | bytes 19486224 | tf_op jit(solution)/shard_map/tre,de->trd/dot_general | solution.py:577
  222.2 9.0 %bitcast_convert_fusion.1 = bf16[768,3072]{1,0:T(8,128)(2,1)} fusion(bf16[2,320,3072]{2,1,0:T(8,128)(2,1)} %get-tuple-element.150, f32[2,320,768]{2,1,0:T(8,128)} %copy-done.7, f32[768]{0:T(1024)} %param.28, f32[768]{0:T(1024)} %param.27, f32[2,320]{1,0:T(2,128)} %copy-done.37, f32[2,320]{1,0:T(2,128)S(1)} %broadcast_multiply_fusion.5), kind=kOutput, calls=%fused_computation.2 | convolution fusion | flops 3024715776 | bytes 10628096 | tf_op jit(solution)/shard_map/trd,tre->de/dot_general | solution.py:576
  231.9 8.2 %bitcast_convert_fusion = bf16[3072,768]{1,0:T(8,128)(2,1)} fusion(bf16[2,320,3072]{2,1,0:T(8,128)(2,1)} %copy-done.15, bf16[2,64,768]{2,1,0:T(8,128)(2,1)} %param.33, bf16[2,256,768]{2,1,0:T(8,128)(2,1)S(1)} %copy-done.28, bf16[2,320]{1,0:T(2,128)(2,1)S(1)} %copy-done.41), kind=kOutput, calls=%fused_computation.1 | convolution fusion | flops 3025207296 | bytes 9635072 | tf_op jit(solution)/shard_map/tre,trd->ed/dot_general | solution.py:572
  244.3 25.9 %swap_rows.7 = bf16[8,480,128]{2,1,0:T(8,128)(2,1)} custom-call(bf16[8,480,128]{2,1,0:T(8,128)(2,1)} %maximum_maximum_fusion.3.src), custom_call_target="tpu_custom_call" | custom-call | tf_op jit(solution)/shard_map/swap_rows/pallas_call | solution.py:322
  274.1 5.8 reshape.328
  284.3 45.4 %attend_back.1 = (bf16[3,2560,64]{2,1,0:T(8,128)(2,1)}, bf16[3,2048,64]{2,1,0:T(8,128)(2,1)S(1)}, bf16[3,2048,64]{2,1,0:T(8,128)(2,1)S(1)}) custom-call(bf16[3,2560,128]{2,1,0:T(8,128)(2,1)} %get-tuple-element.21.q_ref, bf16[3,2048,128]{2,1,0:T(8,128)(2,1)S(1)} %bitcast.156, bf16[3,64,2048]{2,1,0:T(8,128)(2,1)S(1)} %bitcast.159, ...), custom_call_target="tpu_custom_call" | custom-call | tf_op jit(solution)/shard_map/attend_back/pallas_call | solution.py:442
  332.1 2.4 copy.105
  334.5 2.4 copy.104
  345.0 4.1 bitcast_convert_fusion.3
  351.3 24.7 %swap_rows.9 = bf16[8,96,576]{2,1,0:T(8,128)(2,1)} custom-call(bf16[8,96,576]{2,1,0:T(8,128)(2,1)} %bitcast.170), custom_call_target="tpu_custom_call" | custom-call | tf_op jit(solution)/shard_map/swap_rows/pallas_call | solution.py:322
  385.0 11.0 %fusion.1 = (f32[768]{0:T(1024)}, f32[8,320]{1,0:T(8,128)S(1)}, f32[8,320]{1,0:T(8,128)S(1)}, f32[768]{0:T(1024)}, f32[8,320,768,1,1]{2,1,4,0,3:T(8,128)}) fusion(f32[8,320,768]{2,1,0:T(8,128)} %copy-done.5, f32[8,320]{1,0:T(8,128)} %copy-done.32, f32[8,320]{1,0:T(8,128)S(1)} %broadcast_multiply_fusion.2, f32[768]{0:T(1024)S(1)} %copy-done.45, ...), kind=kOutput, calls=%fused_computation.12 | convolution fusion | flops 2285561344 | bytes 19612672 | tf_op jit(solution)/shard_map/pre,de->prd/dot_general | solution.py:603
  395.9 7.3 %reduce-scatter.6.cloned.1.call-done = bf16[96,3072]{1,0:T(8,128)(2,1)} async-done(((bf16[768,3072]{1,0:T(8,128)(2,1)}), bf16[96,3072]{1,0:T(8,128)(2,1)}) %reduce-scatter.6.cloned.1.call-update) | async-done | bytes 589840 | tf_op jit(solution)/shard_map/reduce_scatter | solution.py:474
  403.3 98.8 %reduce-scatter.8.cloned.1.call-done = bf16[384,768]{1,0:T(8,128)(2,1)} async-done(((bf16[3072,768]{1,0:T(8,128)(2,1)}), bf16[384,768]{1,0:T(8,128)(2,1)}) %reduce-scatter.8.cloned.1.call-update) | async-done | bytes 589840 | tf_op jit(solution)/shard_map/reduce_scatter | solution.py:474
  502.2 6.8 multiply_convert_fusion
  512.6 4.2 convolution_convert_fusion.1.src
  516.9 17.0 %swap_rows.8 = bf16[8,320,128]{2,1,0:T(8,128)(2,1)} custom-call(bf16[8,320,128]{2,1,0:T(8,128)(2,1)} %convolution_convert_fusion.1.src), custom_call_target="tpu_custom_call" | custom-call | tf_op jit(solution)/shard_map/swap_rows/pallas_call | solution.py:322
  538.4 2.7 pad_maximum_fusion.1
  541.1 42.3 %all-reduce.6 = (f32[768]{0:T(1024)S(1)}, f32[768]{0:T(1024)S(1)}, f32[768]{0:T(1024)S(1)}, f32[768]{0:T(1024)S(1)}, f32[3072]{0:T(1024)S(1)}, /*index=5*/f32[4]{0:T(128)S(1)}, f32[]{:T(128)}) all-reduce(f32[768]{0:T(1024)S(1)} %copy-done.51, f32[768]{0:T(1024)S(1)} %copy-done.52, ...), channel_id=1, replica_groups=mesh['tab'=4,'row'=8] {'tab','row'}, use_global_device_ids=true, to_apply=%region_11.12 | all-reduce | flops 6149 | bytes 49192 | tf_op jit(solution)/shard_map/psum | solution.py:626
  595.4 90.2 %all-reduce.11.cloned.1.call-done = f32[100,768]{1,0:T(8,128)} async-done(((f32[100,768]{1,0:T(8,128)}), f32[100,768]{1,0:T(8,128)}) %all-reduce.11.cloned.1.call-update) | async-done | bytes 307216 | tf_op jit(solution)/shard_map/psum | solution.py:626
  (235 shorter events, 98.0 us)
Async XLA Ops:
  7.2 138.2 %copy-start = (bf16[768,768]{1,0:T(8,128)(2,1)S(1)}, bf16[768,768]{1,0:T(8,128)(2,1)}, u32[]{:S(2)}) copy-start(bf16[768,768]{1,0:T(8,128)(2,1)} %param.26) | copy-start | bytes 3538948
  7.2 388.7 %reduce-scatter.4.cloned.1.call-start = ((), (), s32[]{:S(2)}) async-start(), calls=%async_computation.4 | async-start | bytes 1327104 | tf_op jit(solution)/shard_map/reduce_scatter | solution.py:474
  13.2 23.2 %copy-start.20 = (bf16[100,768]{1,0:T(8,128)(2,1)S(1)}, bf16[100,768]{1,0:T(8,128)(2,1)}, u32[]{:S(2)}) copy-start(bf16[100,768]{1,0:T(8,128)(2,1)} %param.22) | copy-start | bytes 460804
  14.5 24.3 %copy-start.16 = (bf16[768,3,3,64]{0,3,2,1:T(8,128)(2,1)}, bf16[768,3,3,64]{0,3,2,1:T(8,128)(2,1)S(1)}, u32[]{:S(2)}) copy-start(bf16[768,3,3,64]{0,3,2,1:T(8,128)(2,1)S(1)} %constant_dynamic-slice_fusion) | copy-start | bytes 2654212
  151.1 8.9 %copy-start.37 = (f32[2,320]{1,0:T(2,128)}, f32[2,320]{1,0:T(2,128)S(1)}, u32[]{:S(2)}) copy-start(f32[2,320]{1,0:T(2,128)S(1)} %add_rsqrt_fusion.1) | copy-start | bytes 7684
  151.1 8.9 %copy-start.47 = (s32[256]{0:T(256)}, s32[256]{0:T(256)S(1)}, u32[]{:S(2)}) copy-start(s32[256]{0:T(256)S(1)} %iota_add_fusion) | copy-start | bytes 3076
  151.2 8.8 %copy-start.62 = (s32[64]{0:T(128)}, s32[64]{0:T(128)S(1)}, u32[]{:S(2)}) copy-start(s32[64]{0:T(128)S(1)} %iota_add_fusion.1) | copy-start | bytes 772
  151.4 66.8 %copy-start.40 = (bf16[2,320]{1,0:T(2,128)(2,1)}, bf16[2,320]{1,0:T(2,128)(2,1)S(1)}, u32[]{:S(2)}) copy-start(bf16[2,320]{1,0:T(2,128)(2,1)S(1)} %get-tuple-element.139) | copy-start | bytes 3844
  179.3 8.3 %copy-start.15 = (bf16[2,320,3072]{2,1,0:T(8,128)(2,1)}, bf16[2,320,3072]{2,1,0:T(8,128)(2,1)S(1)}, u32[]{:S(2)}) copy-start(bf16[2,320,3072]{2,1,0:T(8,128)(2,1)S(1)} %get-tuple-element.119) | copy-start | bytes 11796484
  179.3 8.3 %copy-start.28 = (bf16[2,256,768]{2,1,0:T(8,128)(2,1)S(1)}, bf16[2,256,768]{2,1,0:T(8,128)(2,1)}, u32[]{:S(2)}) copy-start(bf16[2,256,768]{2,1,0:T(8,128)(2,1)} %param.32) | copy-start | bytes 2359300
  179.3 8.3 %copy-start.29 = (bf16[2,64,768]{2,1,0:T(8,128)(2,1)S(1)}, bf16[2,64,768]{2,1,0:T(8,128)(2,1)}, u32[]{:S(2)}) copy-start(bf16[2,64,768]{2,1,0:T(8,128)(2,1)} %param.33) | copy-start | bytes 589828
  179.3 8.3 %copy-start.36 = (f32[3072]{0:T(1024)S(1)}, f32[3072]{0:T(1024)}, u32[]{:S(2)}) copy-start(f32[3072]{0:T(1024)} %param.30) | copy-start | bytes 36868
  187.6 19.9 %copy-start.8 = (f32[2,320,768]{2,1,0:T(8,128)S(1)}, f32[2,320,768]{2,1,0:T(8,128)}, u32[]{:S(2)}) copy-start(f32[2,320,768]{2,1,0:T(8,128)} %copy-done.7) | copy-start | bytes 5898244
  187.6 19.9 %copy-start.24 = (f32[2,320,768]{2,1,0:T(8,128)S(1)}, f32[2,320,768]{2,1,0:T(8,128)}, u32[]{:S(2)}) copy-start(f32[2,320,768]{2,1,0:T(8,128)} %copy-done.23) | copy-start | bytes 5898244
  187.6 19.9 %copy-start.38 = (f32[2,320]{1,0:T(2,128)S(1)}, f32[2,320]{1,0:T(2,128)}, u32[]{:S(2)}) copy-start(f32[2,320]{1,0:T(2,128)} %copy-done.37) | copy-start | bytes 7684
  187.6 19.9 %copy-start.43 = (f32[768]{0:T(1024)S(1)}, f32[768]{0:T(1024)}, u32[]{:S(2)}) copy-start(f32[768]{0:T(1024)} %param.27) | copy-start | bytes 9220
  222.2 181.1 %reduce-scatter.6.cloned.1.call-start = ((), (), s32[]{:S(2)}) async-start(), calls=%async_computation.5 | async-start | bytes 5308416 | tf_op jit(solution)/shard_map/reduce_scatter | solution.py:474
  231.2 270.9 %reduce-scatter.8.cloned.1.call-start = ((), (), s32[]{:S(2)}) async-start(), calls=%async_computation.6 | async-start | bytes 5308416 | tf_op jit(solution)/shard_map/reduce_scatter | solution.py:474
  240.2 348.2 %all-reduce.13.cloned.1.call-start = ((), (), s32[]{:S(2)}) async-start(), calls=%async_computation.7 | async-start | bytes 3538944 | tf_op jit(solution)/shard_map/psum | solution.py:470
  339.0 5.1 slice-start
  502.1 183.5 %all-reduce.11.cloned.1.call-start = ((), (), s32[]{:S(2)}) async-start(), calls=%async_computation.3 | async-start | bytes 638976 | tf_op jit(solution)/shard_map/psum | solution.py:626
  502.2 6.9 copy-start.10
  502.2 6.9 copy-start.19
  502.2 8.7 %copy-start.13 = (bf16[8,320,128]{2,1,0:T(8,128)(2,1)S(1)}, bf16[8,320,128]{2,1,0:T(8,128)(2,1)}, u32[]{:S(2)}) copy-start(bf16[8,320,128]{2,1,0:T(8,128)(2,1)} %swap_rows.5) | copy-start | bytes 1966084
  512.6 22.9 %copy-start.46 = (f32[2,100]{1,0:T(2,128)S(1)}, f32[2,100]{1,0:T(2,128)}, u32[]{:S(2)}) copy-start(f32[2,100]{1,0:T(2,128)} %get-tuple-element.141) | copy-start | bytes 2404
  512.6 23.6 %copy-start.27 = (bf16[2,320,768]{2,1,0:T(8,128)(2,1)S(1)}, bf16[2,320,768]{2,1,0:T(8,128)(2,1)}, u32[]{:S(2)}) copy-start(bf16[2,320,768]{2,1,0:T(8,128)(2,1)} %get-tuple-element.126) | copy-start | bytes 2949124
  516.9 24.2 %copy-start.39 = (f32[3072]{0:T(1024)S(1)}, f32[3072]{0:T(1024)}, u32[]{:S(2)}) copy-start(f32[3072]{0:T(1024)} %get-tuple-element.149) | copy-start | bytes 36868
  516.9 24.2 %copy-start.49 = (f32[768]{0:T(1024)S(1)}, f32[768]{0:T(1024)}, u32[]{:S(2)}) copy-start(f32[768]{0:T(1024)} %get-tuple-element.102) | copy-start | bytes 9220
  516.9 24.2 %copy-start.50 = (f32[768]{0:T(1024)S(1)}, f32[768]{0:T(1024)}, u32[]{:S(2)}) copy-start(f32[768]{0:T(1024)} %get-tuple-element.103) | copy-start | bytes 9220
  516.9 24.2 %copy-start.51 = (f32[768]{0:T(1024)S(1)}, f32[768]{0:T(1024)}, u32[]{:S(2)}) copy-start(f32[768]{0:T(1024)} %get-tuple-element.85) | copy-start | bytes 9220
  516.9 24.2 %copy-start.52 = (f32[768]{0:T(1024)S(1)}, f32[768]{0:T(1024)}, u32[]{:S(2)}) copy-start(f32[768]{0:T(1024)} %get-tuple-element.90) | copy-start | bytes 9220
  588.3 6.4 copy-start.30
  (39 other events, 103.5 us)
Sparse Core Ops, SparseCore 0:
  222.3 73.4 reduce-scatter.3
  299.4 103.7 reduce-scatter.5
  406.9 95.1 reduce-scatter.7
  504.6 46.6 all-reduce.12
  557.9 127.6 all-reduce.10
